TPU v7x, 128 devices: a whole 4x4x4 slice. The times are simulated.
128 devices in a mesh: row: 4 (over z), kv: 32 (over x, y, core).
Axes of the slice: x: 4, y: 4, z: 4, core: 2. Of those that a mesh axis runs over, the one named last changes fastest.
Arguments:
- query: bfloat16 [8, 128, 576], P('row')
- latent_cache: bfloat16 [8, 163840, 576], P('row', 'kv')
- new_latent: bfloat16 [8, 576], P('row'), may hold values from -12 to 12
- lengths: int32 [8], P('row'), may hold values from 20480 to 163840, as said below
- w_uv: bfloat16 [128, 512, 128], P('kv'), may hold values from -0.25 to 0.25
- w_o: bfloat16 [16384, 7168], P('kv'), may hold values from -0.046875 to 0.046875
- hidden_in: bfloat16 [8, 7168], P('row'), may hold values from -0.59765625 to 0.59765625
- norm_gain: bfloat16 [7168], replicated, may hold values from 0.099609375 to 1.8984375
- w_gate: bfloat16 [7168, 18432], P(None, ('row', 'kv')), may hold values from -0.0625 to 0.0625
- w_up: bfloat16 [7168, 18432], P(None, ('row', 'kv')), may hold values from -0.0625 to 0.0625
- w_down: bfloat16 [18432, 7168], P(('row', 'kv')), may hold values from -0.15625 to 0.15625
Outputs:
- layer_out: float32 [8, 7168], P('row', 'kv')
Inputs may be any that keep to these rules, and one draw needn't show every extreme that they name: `lengths`: each row's count of filled cache positions, each between 20480 and 163840; some row fills all 163840.
All inputs are finite; a program needn't handle non-finite values.
Results may differ from a plain program's by a relative error of at most 0.035.
Values may be sent and summed in bfloat16 or wider, within the bound.
A program may use at most 128 MiB of HBM per device.

v0:
```python
import jax
import jax.numpy as jnp
from jax import lax
from jax.sharding import PartitionSpec as P

ROPE = 64
HEAD_DIM = 128


NEG_FILL = -1e30


def combined_all(x, axis, combine):
    everything = jax.tree.map(lambda part: lax.all_gather(part, axis), x)
    first = jax.tree.map(lambda part: part[0], everything)

    def lap(k, so_far):
        return combine(so_far, jax.tree.map(lambda part: part[k], everything))

    return lax.fori_loop(1, lax.axis_size(axis), lap, first)


def combine_parts(first_part, second_part):
    top_a, total_a, weighted_a = first_part
    top_b, total_b, weighted_b = second_part
    peak_score = jnp.maximum(top_a, top_b)
    factor_a = jnp.exp(top_a - peak_score)
    factor_b = jnp.exp(top_b - peak_score)
    return (
        peak_score,
        total_a * factor_a + total_b * factor_b,
        weighted_a * factor_a[..., None] + weighted_b * factor_b[..., None],
    )


def body(
    query, latent_cache, new_latent, lengths, w_uv, w_o, hidden_in, norm_gain, w_gate, w_up, w_down
):
    rows_here, span_len, entry_len = latent_cache.shape
    latent = w_uv.shape[1]
    local_heads = w_uv.shape[0]
    kv_count = lax.axis_size("kv")
    row_count = lax.axis_size("row")
    kv_index = lax.axis_index("kv")
    row_index = lax.axis_index("row")
    score_scale = (HEAD_DIM + ROPE) ** (-0.5)
    first_pos = kv_index * span_len
    new_score = (
        jnp.einsum("rhq,rq->rh", query, new_latent, preferred_element_type=jnp.float32)
        * score_scale
    )
    new_value = new_latent[:, :latent].astype(jnp.float32)
    scores = (
        jnp.einsum("rhq,rpq->rhp", query, latent_cache, preferred_element_type=jnp.float32)
        * score_scale
    )
    valid = ((first_pos + jnp.arange(span_len))[None, :] < lengths[:, None])[:, None, :]
    top_score = jnp.max(jnp.where(valid, scores, NEG_FILL), axis=-1)
    weights = jnp.where(valid, jnp.exp(scores - top_score[..., None]), 0.0).astype(jnp.bfloat16)
    total = jnp.sum(weights.astype(jnp.float32), axis=-1)
    weighted = jnp.einsum(
        "rhp,rpl->rhl", weights, latent_cache[:, :, :latent], preferred_element_type=jnp.float32
    )
    first_head = kv_index * local_heads
    own_new = lax.dynamic_slice_in_dim(new_score, first_head, local_heads, 1)
    merged_top, merged_total, merged_weighted = combined_all(
        (top_score, total, weighted), "kv", combine_parts
    )
    merged_top = lax.dynamic_slice_in_dim(merged_top, first_head, local_heads, 1)
    merged_total = lax.dynamic_slice_in_dim(merged_total, first_head, local_heads, 1)
    merged_weighted = lax.dynamic_slice_in_dim(merged_weighted, first_head, local_heads, 1)
    own_peak = jnp.maximum(merged_top, own_new)
    rescale = jnp.exp(merged_top - own_peak)
    own_weight = jnp.exp(own_new - own_peak)
    head_total = merged_total * rescale + own_weight
    head_weighted = (
        merged_weighted * rescale[..., None] + own_weight[..., None] * new_value[:, None, :]
    )
    attended = (head_weighted / head_total[..., None]).astype(jnp.bfloat16)
    head_values = jnp.einsum(
        "rhl,hld->rhd", attended, w_uv, preferred_element_type=jnp.float32
    ).astype(jnp.bfloat16)
    flat_values = head_values.reshape(rows_here, local_heads * head_values.shape[2])
    partial_value = jnp.dot(flat_values, w_o, preferred_element_type=jnp.float32)
    model_width = partial_value.shape[1]
    feat_width = model_width // kv_count
    attn = lax.psum(partial_value, "kv")
    stream = (hidden_in.astype(jnp.float32) + attn).astype(jnp.bfloat16)
    whole_stream = lax.all_gather(stream, "row", axis=0, tiled=True)
    stream_f = whole_stream.astype(jnp.float32)
    mean_sq = jnp.mean(stream_f * stream_f, axis=1, keepdims=True)
    normed = (
        stream_f * lax.rsqrt(mean_sq + 1e-06) * norm_gain.astype(jnp.float32)[None, :]
    ).astype(jnp.bfloat16)
    gate_proj = jnp.dot(normed, w_gate, preferred_element_type=jnp.float32)
    up_proj = jnp.dot(normed, w_up, preferred_element_type=jnp.float32)
    hidden = (jax.nn.silu(gate_proj) * up_proj).astype(jnp.bfloat16)
    down_proj = jnp.dot(hidden, w_down, preferred_element_type=jnp.float32)
    term_blocks = down_proj.reshape(row_count, rows_here, kv_count, feat_width).transpose(
        0, 2, 1, 3
    )
    term_blocks = term_blocks.reshape(row_count * kv_count, rows_here, feat_width)
    summed = lax.psum_scatter(term_blocks, ("row", "kv"), scatter_dimension=0, tiled=True)[0]
    own_stream = lax.dynamic_slice(
        stream_f, (row_index * rows_here, kv_index * feat_width), (rows_here, feat_width)
    )
    return own_stream + summed


def solution(mesh):
    placed = (
        P("row", None, None),
        P("row", "kv", None),
        P("row", None),
        P("row"),
        P("kv", None, None),
        P("kv", None),
        P("row", None),
        P(),
        P(None, ("row", "kv")),
        P(None, ("row", "kv")),
        P(("row", "kv"), None),
    )
    return jax.shard_map(
        body, mesh=mesh, in_specs=placed, out_specs=P("row", "kv"), check_vma=False
    )
```

profile of v0, /device:TPU:1, one launch (start us, length us, event | category | flops | bytes accessed | tf_op | source)
XLA Modules:
  0.0 436.2 jit_solution(13148348031356534303)
XLA Ops:
  6.5 0.0 copy-start
  6.5 0.0 all-gather.8.cloned.1.call-start
  6.5 0.9 broadcast_compare_fusion
  7.4 7.1 %select_reduce_fusion = (f32[2,128]{1,0:T(2,128)S(1)}, f32[2,128,5120]{2,1,0:T(8,128)S(1)}) fusion(pred[2,5120]{1,0:T(4,128)(4,1)S(1)} %broadcast_compare_fusion, bf16[2,128,576]{1,2,0:T(8,128)(2,1)} %param.13, bf16[2,5120,576]{1,2,0:T(8,128)(2,1)} %param.14), kind=kOutput, calls=%fused_computation.14 | convolution fusion | flops 1513881344 | bytes 17345536 | tf_op jit(solution)/shard_map/rhq,rpq->rhp/dot_general | solution.py:54
  14.6 2.3 copy-done.1
  16.9 7.2 %fusion.3 = f32[2,128,512]{2,1,0:T(8,128)} fusion(bf16[2,5120,576]{1,2,0:T(8,128)(2,1)} %param.14, f32[2,128,5120]{2,1,0:T(8,128)S(1)} %get-tuple-element.208, f32[2,128]{1,0:T(2,128)S(1)} %get-tuple-element.207, pred[2,5120]{1,0:T(4,128)(4,1)S(1)} %broadcast_compare_fusion), kind=kOutput, calls=%fused_computation.9 | convolution fusion | flops 1346109440 | bytes 16264192 | tf_op jit(solution)/shard_map/rhp,rpl->rhl/dot_general | solution.py:61
  24.1 0.0 all-gather.8.cloned.1.call-update
  24.1 0.0 all-reduce.3.cloned.1.call-start
  24.2 0.0 copy-done.6
  24.2 25.8 %all-gather.3 = f32[32,2,128]{2,1,0:T(2,128)S(1)} all-gather(f32[1,2,128]{2,1,0:T(2,128)S(1)} %bitcast.55), channel_id=2, replica_groups=mesh['row'=4,'kv'=32] {'kv'}, dimensions={0}, use_global_device_ids=true | all-gather | bytes 33792 | tf_op jit(solution)/shard_map/all_gather | solution.py:14
  50.0 3.6 convert_reduce_fusion
  53.6 23.7 %all-gather.4 = f32[32,2,128]{2,1,0:T(2,128)S(1)} all-gather(f32[1,2,128]{2,1,0:T(2,128)S(1)} %bitcast.57), channel_id=3, replica_groups=mesh['row'=4,'kv'=32] {'kv'}, dimensions={0}, use_global_device_ids=true | all-gather | bytes 33792 | tf_op jit(solution)/shard_map/all_gather | solution.py:14
  77.3 0.0 copy-done.2
  77.3 0.2 fusion.18
  77.5 22.8 %all-gather.8.cloned.1.call-done = f32[64,128,512]{2,1,0:T(8,128)} async-done(((f32[2,128,512]{2,1,0:T(8,128)}), f32[64,128,512]{2,1,0:T(8,128)}) %all-gather.8.cloned.1.call-update) | async-done | bytes 16777232 | tf_op jit(solution)/shard_map/all_gather | solution.py:14
  100.3 1.1 slice.27
  101.4 39.3 %while.19 = (s32[]{:T(128)}, f32[2,128]{1,0:T(2,128)S(1)}, f32[2,128]{1,0:T(2,128)S(1)}, f32[2,128,512]{2,1,0:T(8,128)S(1)}, f32[32,2,128]{2,1,0:T(2,128)S(1)}, ...) while((s32[]{:T(128)}, f32[2,128]{1,0:T(2,128)S(1)}, ...), condition=%wide.region_3.4_spmd, body=%wide.region_2.3_spmd.sunk | while | flops 394757 | bytes 1583255 | solution.py:20
  101.4 1.2 fusion.41
  102.7 1.2 fusion.41
  104.0 1.2 fusion.41
  105.2 1.2 fusion.41
  106.5 1.2 fusion.41
  107.8 1.2 fusion.41
  109.0 1.2 fusion.41
  110.3 1.2 fusion.41
  111.6 1.2 fusion.41
  112.8 1.2 fusion.41
  114.1 1.2 fusion.41
  115.4 1.2 fusion.41
  116.7 1.2 fusion.41
  117.9 1.2 fusion.41
  119.2 1.2 fusion.41
  120.5 1.2 fusion.41
  121.7 1.2 fusion.41
  123.0 1.2 fusion.41
  124.3 1.2 fusion.41
  125.5 1.2 fusion.41
  126.8 1.2 fusion.41
  128.1 1.2 fusion.41
  129.3 1.2 fusion.41
  130.6 1.2 fusion.41
  131.9 1.2 fusion.41
  133.1 1.2 fusion.41
  134.4 1.2 fusion.41
  135.7 1.2 fusion.41
  136.9 1.2 fusion.41
  138.2 1.2 fusion.41
  139.5 1.2 fusion.41
  140.7 0.0 copy-start.4
  140.7 0.1 multiply_add_fusion
  140.8 0.1 fusion.10
  140.9 0.0 copy-done.3
  140.9 4.3 fusion.8
  145.1 121.2 %psum.7 = f32[2,7168]{1,0:T(2,128)S(1)} all-reduce(f32[2,7168]{1,0:T(2,128)S(1)} %fusion.8), channel_id=1, replica_groups=mesh['row'=4,'kv'=32] {'kv'}, use_global_device_ids=true, to_apply=%region_4.5 | all-reduce | flops 14336 | bytes 114688 | tf_op jit(solution)/shard_map/psum | solution.py:87
  266.3 0.0 copy-done.4
  266.4 9.8 %all-gather.5 = bf16[4,2,7168]{2,1,0:T(2,128)(2,1)S(1)} all-gather(bf16[1,2,7168]{2,1,0:T(2,128)(2,1)S(1)} %fusion.9), channel_id=1, replica_groups=mesh['row'=4,'kv'=32] {'row'}, dimensions={0}, use_global_device_ids=true | all-gather | bytes 143360 | tf_op jit(solution)/shard_map/all_gather | solution.py:89
  276.2 0.2 multiply_reduce_fusion
  276.4 2.2 fusion.26
  278.7 3.2 fusion.6
  281.8 0.2 reshape.53
  282.0 0.9 copy.17
  282.9 0.0 all-reduce.3.cloned.1.call-update
  283.0 145.0 %all-reduce.3.cloned.1.call-done = f32[128,2,224]{2,1,0:T(2,128)} async-done(((f32[128,2,224]{2,1,0:T(2,128)}), f32[128,2,224]{2,1,0:T(2,128)}) %all-reduce.3.cloned.1.call-update) | async-done | bytes 229392
  428.0 1.3 fusion.21
  (47 shorter events, 1.0 us)
Async XLA Ops:
  6.5 272.1 %copy-start = (bf16[144,7168]{1,0:T(8,128)(2,1)S(1)}, bf16[144,7168]{1,0:T(8,128)(2,1)}, u32[]{:S(2)}) copy-start(bf16[144,7168]{1,0:T(8,128)(2,1)} %param.23) | copy-start | bytes 6193156
  6.5 93.8 %all-gather.8.cloned.1.call-start = ((), (), s32[]{:S(2)}) async-start(), calls=%async_computation | async-start | bytes 17301504 | tf_op jit(solution)/shard_map/all_gather | solution.py:14
  14.6 2.3 copy-start.1
  16.9 7.3 %copy-start.6 = (bf16[7168]{0:T(1024)(128)(2,1)S(1)}, bf16[7168]{0:T(1024)(128)(2,1)}, u32[]{:S(2)}) copy-start(bf16[7168]{0:T(1024)(128)(2,1)} %param.20) | copy-start | bytes 43012
  24.1 53.2 %copy-start.2 = (bf16[2,128,576]{1,2,0:T(8,128)(2,1)S(1)}, bf16[2,128,576]{1,2,0:T(8,128)(2,1)}, u32[]{:S(2)}) copy-start(bf16[2,128,576]{1,2,0:T(8,128)(2,1)} %param.13) | copy-start | bytes 884740
  24.1 53.2 %copy-start.5 = (bf16[2,576]{1,0:T(2,128)(2,1)S(1)}, bf16[2,576]{1,0:T(2,128)(2,1)}, u32[]{:S(2)}) copy-start(bf16[2,576]{1,0:T(2,128)(2,1)} %param.15) | copy-start | bytes 6916
  24.1 403.9 %all-reduce.3.cloned.1.call-start = ((), (), s32[]{:S(2)}) async-start(), calls=%async_computation.1 | async-start | bytes 524288
  53.6 87.3 %copy-start.3 = (bf16[4,512,128]{2,1,0:T(8,128)(2,1)S(1)}, bf16[4,512,128]{2,1,0:T(8,128)(2,1)}, u32[]{:S(2)}) copy-start(bf16[4,512,128]{2,1,0:T(8,128)(2,1)} %param.17) | copy-start | bytes 1572868
  140.7 125.6 %copy-start.4 = (bf16[2,7168]{1,0:T(2,128)(2,1)S(1)}, bf16[2,7168]{1,0:T(2,128)(2,1)}, u32[]{:S(2)}) copy-start(bf16[2,7168]{1,0:T(2,128)(2,1)} %param.19) | copy-start | bytes 86020
Sparse Core Ops, SparseCore 0:
  24.2 76.0 all-gather.7
  283.1 144.8 all-reduce.2
where the time goes:
time: 438 us; the launch traced here: 436 us
  blocking collectives  180 us (41%)
  waiting for transfers between devices  168 us (38%)
  other arithmetic  44.7 us (10%)
  matrix products  24.1 us (6%)
  between operations  13.5 us (3%)
  local copies, waits for them, and re-layouts  4.53 us (1%)
    unnamed x3, waiting for transfers between devices  145 us
    psum x1, blocking collectives, body(): attn = lax.psum(partial_value, 'kv')  121 us
    all_gather x2, blocking collectives, combined_all(): everything = jax.tree.map(lambda part: lax.all_gather(part, axis), x)  49.5 us
    add x31, other arithmetic, combine_parts(): weighted_a * factor_a[..., None] + weighted_b * factor_b[..., None]  37.5 us
    all_gather x1, waiting for transfers between devices, combined_all(): everything = jax.tree.map(lambda part: lax.all_gather(part, axis), x)  22.8 us
    all_gather x1, blocking collectives, body(): whole_stream = lax.all_gather(stream, 'row', axis=0, tiled=True)  9.84 us
  transfers between devices with their start and end apart: 2, of which 2 were waited for; matrix products, arithmetic and copies ran while one was open for 1% of the time, Pallas kernels for 0%

commit v1 on v0

v1 whole, which is shorter than its diff:
```python
import jax
import jax.numpy as jnp
from jax import lax
from jax.experimental import pallas as pl
from jax.experimental.pallas import tpu as pltpu
from jax.sharding import PartitionSpec as P

LOGICAL = pl.DeviceIdType.LOGICAL
F32, BF16 = jnp.float32, jnp.bfloat16

HEADS, LATENT, ROPE, HEAD_DIM, QK = 128, 512, 64, 128, 576
D, LOCAL_FF, SPAN = 7168, 144, 5120
KV, ROWS, HERE = 32, 4, 2
OUT_COLS = D // KV
CHUNK = 1024
CHUNKS = SPAN // CHUNK
REDUCERS = 14
LOG2E = 1.4426950408889634
SCALE2 = LOG2E * (HEAD_DIM + ROPE) ** -0.5
NEG_FILL = -1e30


def dot(a, b, dims=((1,), (0,))):
    return lax.dot_general(a, b, (dims, ((), ())), preferred_element_type=F32)


def kernel(
    q_hbm, cache_hbm, new_hbm, lengths_ref, uv_hbm, wo_hbm, hid_hbm, gain_hbm, gate_hbm, up_hbm, down_hbm,
    out_ref,
    qt, kt, new, uv, wo, hid_in, gain, wg, wu, wd,
    q, s, w, acc, hid_tiles,
    part_out, part_in, attn_out, attn_in, row_tiles, stream_own, stream_all, wide,
    down_out, down_in, last_own, last_in, wide_stream,
    in_sem, cache_sem, send_sem, recv_sem,
):
    k = lax.axis_index("kv")
    z = lax.axis_index("row")

    small = [
        pltpu.make_async_copy(src, dst, in_sem.at[i])
        for i, (src, dst) in enumerate(((q_hbm, qt), (new_hbm, new), (hid_hbm, hid_in), (gain_hbm, gain)))
    ]
    for copy in small:
        copy.start()
    cache = [
        [
            pltpu.make_async_copy(
                cache_hbm.at[r, :, pl.ds(c * CHUNK, CHUNK)], kt.at[r, :, pl.ds(c * CHUNK, CHUNK)], cache_sem.at[r, c]
            )
            for c in range(CHUNKS)
        ]
        for r in range(HERE)
    ]
    for r in range(HERE):
        for c in range(CHUNKS):
            cache[r][c].start()
    weights = [
        pltpu.make_async_copy(src, dst, in_sem.at[4 + i])
        for i, (src, dst) in enumerate(((uv_hbm, uv), (wo_hbm, wo), (gate_hbm, wg), (up_hbm, wu), (down_hbm, wd)))
    ]

    barrier = pltpu.get_barrier_semaphore()

    plane = z * KV
    own_chip, own_core = lax.div(k, 2), lax.rem(k, 2)
    xs = [4 * lax.rem(lax.div(own_chip, 4) + d, 4) for d in range(4)]
    ys = [lax.rem(lax.rem(own_chip, 4) + d, 4) for d in range(4)]
    cores = [own_core, 1 - own_core]
    offsets = sorted(((dx, dy) for dx in range(4) for dy in range(4)), key=lambda o: -min(o[0], 4 - o[0]) - min(o[1], 4 - o[1]))
    chips = [xs[dx] + ys[dy] for dx, dy in offsets]
    peers = [2 * chip + core for chip in chips for core in cores]
    del peers[-2]
    row_peers = [lax.rem(z + d, ROWS) * KV + k for d in (2, 1, 3)]
    for peer in [plane + p for p in peers] + row_peers:
        pl.semaphore_signal(barrier, inc=1, device_id=peer, device_id_type=LOGICAL)

    def send(src, dst, lane, device):
        pltpu.make_async_remote_copy(
            src_ref=src, dst_ref=dst, send_sem=send_sem.at[lane], recv_sem=recv_sem.at[lane],
            device_id=device, device_id_type=LOGICAL,
        ).start()

    def send_kv(src, dst, lane):
        for peer in peers:
            send(src(peer), dst, lane, plane + peer)

    def send_row(src, dst, lane):
        for peer in row_peers:
            send(src, dst, lane, peer)

    def wait_for(sem, buffer, count):
        span = buffer.at[pl.ds(0, count)]
        pltpu.make_async_copy(span, span, sem).wait()

    sub = lax.broadcasted_iota(jnp.int32, (8, 128), 0)
    lane = lax.broadcasted_iota(jnp.int32, (8, 128), 1)

    for copy in small:
        copy.wait()
    new_score = []
    for r in range(HERE):
        q_f = qt[r].astype(F32).T
        q[r] = q_f.astype(BF16)
        new_score.append(jnp.sum(q_f * new[r : r + 1, :].astype(F32), axis=1, keepdims=True) * SCALE2)
    def packed(rows, j):
        base = 512 * j
        tile = rows[:, base : base + 128]
        for c in range(1, 4):
            tile = jnp.where(sub // 2 == c, rows[:, base + 128 * c : base + 128 * (c + 1)], tile)
        return tile

    position = lax.broadcasted_iota(jnp.int32, (1, CHUNK), 1) + k * SPAN

    def scores(r, c):
        cache[r][c].wait()
        cols = pl.ds(c * CHUNK, CHUNK)
        raw = dot(q[r], kt[r, :, cols]) * SCALE2
        raw = jnp.where(position + c * CHUNK < lengths_ref[r], raw, NEG_FILL)
        s[r, :, cols] = raw
        return jnp.max(raw, axis=1, keepdims=True)

    def weigh(r, c, top):
        cols = pl.ds(c * CHUNK, CHUNK)
        value = jnp.exp2(s[r, :, cols] - top)
        w[r, :, cols] = value.astype(BF16)
        return jnp.sum(value, axis=1, keepdims=True)

    def pv(r, c):
        cols = pl.ds(c * CHUNK, CHUNK)
        part = dot(w[r, :, cols], kt[r, :LATENT, cols], ((1,), (1,)))
        if c == 0:
            acc[r] = part
        else:
            acc[r] += part

    top = list(new_score)
    total = [jnp.zeros((HEADS, 1), F32)] * HERE
    for c in range(CHUNKS):
        top[0] = jnp.maximum(top[0], scores(0, c))
    weights[0].start()
    weights[1].start()
    for c in range(CHUNKS):
        top[1] = jnp.maximum(top[1], scores(1, c))
        total[0] = total[0] + weigh(0, c, top[0])
    for copy in weights[2:]:
        copy.start()
    for c in range(CHUNKS):
        pv(0, c)
        total[1] = total[1] + weigh(1, c, top[1])
    for c in range(CHUNKS):
        pv(1, c)

    half = lax.broadcasted_iota(jnp.int32, (16, 8, 128), 1) < 4
    left = lax.broadcasted_iota(jnp.int32, (HEADS, 128), 1) < 64
    wide_zero = jnp.zeros((HEADS, 128), F32)

    def share(first, second):
        t0, t1 = first.reshape(16, 8, 128), second.reshape(16, 8, 128)
        return jnp.where(half, t0, pltpu.roll(t1, 4, 1)), jnp.where(half, pltpu.roll(t0, 4, 1), t1)

    def rounded(value):
        return value.astype(BF16).astype(F32)

    logs = []
    for r in range(HERE):
        own_new = jnp.where(k == 0, jnp.exp2(new_score[r] - top[r]), 0.0)
        norm = jnp.maximum(total[r] + own_new, 1e-30)
        log_total = top[r] + jnp.log(norm) * LOG2E
        high = rounded(log_total)
        middle = rounded(log_total - high)
        low = log_total - high - middle
        logs.append(share(jnp.where(left, high, middle), jnp.where(left, low, wide_zero)))
        mine = (acc[r] + own_new * new[r : r + 1, :LATENT].astype(F32)) * (1.0 / norm)
        quarters = [mine[:, 128 * c : 128 * c + 128] for c in range(4)]
        both = [share(quarters[2 * u], quarters[2 * u + 1]) for u in range(2)]
        for core in range(2):
            part_out[:, core, r] = jnp.concatenate([both[0][core], both[1][core]], axis=1).astype(BF16)
    for core in range(2):
        part_out[:, core, HERE] = jnp.concatenate([logs[0][core], logs[1][core]], axis=1).astype(BF16)
    pl.semaphore_wait(barrier, KV - 1 + ROWS - 1)
    send_kv(lambda peer: part_out.at[lax.div(peer, 2), lax.rem(peer, 2)], part_in.at[k], 1)
    part_in[k] = part_out[own_chip, own_core]

    hid_f = hid_in[...].astype(F32)
    hid_rows = jnp.where(lax.broadcasted_iota(jnp.int32, (8, D), 0) % 2 == 0, hid_f[0:1], hid_f[1:2])

    for j in range(REDUCERS):
        hid_tiles[j] = packed(hid_rows, j)

    wait_for(recv_sem.at[1], part_in, KV - 1)
    weights[0].wait()
    att = []
    for r in range(HERE):
        log_parts = part_in[:, HERE, 8 * r : 8 * r + 8].astype(F32)
        log_parts = log_parts + pltpu.roll(log_parts, 64, 2)
        log_parts = log_parts + pltpu.roll(log_parts, 4, 1)
        factor = jnp.exp2(log_parts - jnp.max(log_parts, axis=0)[None])
        factor = factor * (1.0 / jnp.sum(factor, axis=0))[None]
        data = part_in[:, r].astype(F32)
        att.append([jnp.sum(data[:, 8 * u : 8 * u + 8] * factor, axis=0) for u in range(2)])
    pieces = []
    for c in range(4):
        lo, hi = att[0][c // 2], att[1][c // 2]
        if c % 2 == 0:
            pieces.append(jnp.where(sub < 4, lo, pltpu.roll(hi, 4, 0)))
        else:
            pieces.append(jnp.where(sub < 4, pltpu.roll(lo, 4, 0), hi))
    attended = jnp.concatenate(pieces, axis=1).astype(BF16)
    values = []
    for h in range(4):
        got = dot(attended, uv[h])
        values.append(jnp.where(sub % 2 == 0, got[h : h + 1], got[4 + h : 5 + h]))
    head_values = jnp.concatenate(values, axis=1).astype(BF16)
    weights[1].wait()
    partial = dot(head_values, wo[...])
    for j in range(REDUCERS):
        attn_out[j] = packed(partial, j)

    for chip in chips:

        @pl.when(jnp.logical_and(chip < REDUCERS, k != 2 * chip))
        def _(chip=chip):
            send(attn_out.at[chip], attn_in.at[k], 2, plane + 2 * chip)

    reducer = jnp.logical_and(k % 2 == 0, k < 2 * REDUCERS)

    @pl.when(reducer)
    def _():
        j = own_chip
        attn_in[k] = attn_out[j]
        own_hid = hid_tiles[j]
        wait_for(recv_sem.at[2], attn_in, KV - 1)
        mine = (jnp.sum(attn_in[...], axis=0) + own_hid).astype(BF16).astype(F32)
        row_tiles[z] = mine
        stream_own[...] = mine
        send_row(stream_own, row_tiles.at[z], 3)
        wait_for(recv_sem.at[3], row_tiles, ROWS - 1)
        tiles = []
        for c in range(4):
            tile = None
            for zz in range(ROWS):
                shift = (2 * zz - 2 * c) % 8
                piece = row_tiles[zz]
                if shift:
                    piece = pltpu.roll(piece, shift, 0)
                tile = piece if tile is None else jnp.where(sub // 2 == zz, piece, tile)
            tiles.append(tile)
        for u in range(2):
            both = jnp.concatenate(tiles[2 * u : 2 * u + 2], axis=0).astype(BF16)
            wide[u] = both
            stream_all[j, u] = both
        send_kv(lambda peer: wide, stream_all.at[j], 4)
        wait_for(recv_sem.at[4], stream_all, REDUCERS - 1)

    @pl.when(jnp.logical_not(reducer))
    def _():
        wait_for(recv_sem.at[4], stream_all, REDUCERS)

    parts = stream_all[...].astype(F32)
    stream = jnp.concatenate(
        [parts[t // 4, (t // 2) % 2, 8 * (t % 2) : 8 * (t % 2) + 8] for t in range(D // 128)], axis=1
    )
    mean_sq = jnp.sum(stream * stream, axis=1, keepdims=True) * (1.0 / D)
    normed = (stream * lax.rsqrt(mean_sq + 1e-06) * gain[...].astype(F32).reshape(1, D)).astype(BF16)
    for copy in weights[2:4]:
        copy.wait()
    gate_proj = dot(normed, wg[...], ((1,), (1,)))
    up_proj = dot(normed, wu[...], ((1,), (1,)))
    hidden = (gate_proj / (1.0 + jnp.exp(-gate_proj)) * up_proj).astype(BF16)
    weights[4].wait()
    down = dot(hidden, wd[...])
    down = jnp.concatenate([down, jnp.zeros((8, 128), F32)], axis=1)
    for p in range(KV):
        tile, shift = divmod(OUT_COLS * p, 128)
        three = [down[:, 128 * (tile + i) : 128 * (tile + i + 1)] for i in range(3)]
        if shift:
            turned = [pltpu.roll(t, 128 - shift, 1) for t in three]
            two = [jnp.where(lane < 128 - shift, turned[i], turned[i + 1]) for i in range(2)]
        else:
            two = three[:2]
        down_out[p] = jnp.concatenate(two, axis=0).astype(BF16)
    down_in[k] = down_out[k]
    send_kv(lambda peer: down_out.at[peer], down_in.at[k], 5)

    own_tile = lax.div(7 * k, 4)
    wide_stream[:, pl.ds(0, D)] = stream
    wide_stream[:, pl.ds(D, 512)] = jnp.zeros((8, 512), F32)
    own_stream = wide_stream[:, pl.ds(pl.multiple_of(own_tile * 128, 128), 512)]
    own_stream = pltpu.roll(own_stream, lax.rem(512 - (OUT_COLS * k - 128 * own_tile), 512), 1)[:, :256]

    wait_for(recv_sem.at[5], down_in, KV - 1)
    mine = jnp.sum(down_in[...].astype(F32), axis=0)
    last_own[...] = mine
    last_in[z] = mine
    send_row(last_own, last_in.at[z], 6)
    wait_for(recv_sem.at[6], last_in, ROWS - 1)
    summed = jnp.sum(last_in[...], axis=0)
    result = jnp.concatenate([summed[0:8], summed[8:16]], axis=1) + own_stream
    own = result[0:2]
    for zz in range(1, ROWS):
        own = jnp.where(z == zz, result[2 * zz : 2 * zz + 2], own)
    out_ref[...] = own[:, :OUT_COLS]

    for i, buffer in ((1, part_in), (5, down_in)):
        wait_for(send_sem.at[i], buffer, KV - 1)
    wait_for(send_sem.at[6], last_in, ROWS - 1)

    @pl.when(reducer)
    def _():
        wait_for(send_sem.at[2], attn_out, REDUCERS - 1)
        wait_for(send_sem.at[3], row_tiles, ROWS - 1)
        sent = s.at[0, pl.ds(0, 16), pl.ds(0, 128 * (KV - 1))]
        pltpu.make_async_copy(sent, sent, send_sem.at[4]).wait()

    @pl.when(jnp.logical_not(reducer))
    def _():
        wait_for(send_sem.at[2], attn_out, REDUCERS)


def body(query, latent_cache, new_latent, lengths, w_uv, w_o, hidden_in, norm_gain, w_gate, w_up, w_down):
    anywhere = pl.BlockSpec(memory_space=pl.ANY)
    vmem = pltpu.VMEM
    return pl.pallas_call(
        kernel,
        out_shape=jax.ShapeDtypeStruct((HERE, OUT_COLS), F32),
        in_specs=[anywhere] * 3 + [pl.BlockSpec(memory_space=pltpu.SMEM)] + [anywhere] * 7,
        out_specs=pl.BlockSpec(memory_space=vmem),
        scratch_shapes=[
            vmem((HERE, QK, HEADS), BF16),
            vmem((HERE, QK, SPAN), BF16),
            vmem((HERE, QK), BF16),
            vmem((4, LATENT, HEAD_DIM), BF16),
            vmem((4 * HEAD_DIM, D), BF16),
            vmem((HERE, D), BF16),
            vmem((D,), BF16),
            vmem((LOCAL_FF, D), BF16),
            vmem((LOCAL_FF, D), BF16),
            vmem((LOCAL_FF, D), BF16),
            vmem((HERE, HEADS, QK), BF16),
            vmem((HERE, HEADS, SPAN), F32),
            vmem((HERE, HEADS, SPAN), BF16),
            vmem((HERE, HEADS, LATENT), F32),
            vmem((REDUCERS, 8, 128), F32),
            vmem((KV // 2, 2, HERE + 1, 16, 128), BF16),
            vmem((KV, HERE + 1, 16, 128), BF16),
            vmem((REDUCERS, 8, 128), F32),
            vmem((KV, 8, 128), F32),
            vmem((ROWS, 8, 128), F32),
            vmem((8, 128), F32),
            vmem((REDUCERS, 2, 16, 128), BF16),
            vmem((2, 16, 128), BF16),
            vmem((KV, 16, 128), BF16),
            vmem((KV, 16, 128), BF16),
            vmem((16, 128), F32),
            vmem((ROWS, 16, 128), F32),
            vmem((8, D + 512), F32),
            pltpu.SemaphoreType.DMA((9,)),
            pltpu.SemaphoreType.DMA((HERE, CHUNKS)),
            pltpu.SemaphoreType.DMA((7,)),
            pltpu.SemaphoreType.DMA((7,)),
        ],
        compiler_params=pltpu.CompilerParams(
            collective_id=0, has_side_effects=True, vmem_limit_bytes=60 * 1024 * 1024
        ),
    )(
        jnp.swapaxes(query, 1, 2),
        jnp.swapaxes(latent_cache, 1, 2),
        new_latent,
        lengths,
        w_uv,
        w_o,
        hidden_in,
        norm_gain,
        w_gate.T,
        w_up.T,
        w_down,
    )


def solution(mesh):
    placed = (
        P("row", None, None),
        P("row", "kv", None),
        P("row", None),
        P("row"),
        P("kv", None, None),
        P("kv", None),
        P("row", None),
        P(),
        P(None, ("row", "kv")),
        P(None, ("row", "kv")),
        P(("row", "kv"), None),
    )
    return jax.shard_map(body, mesh=mesh, in_specs=placed, out_specs=P("row", "kv"), check_vma=False)
```

time: 438 us -> 51.3 us (0.12)
  blocking collectives: 180 us -> 0 us
  waiting for transfers between devices: 168 us -> 0 us
  Pallas kernels: 0 us -> 49.9 us
  other arithmetic: 44.7 us -> 0 us
  matrix products: 24.1 us -> 0 us
  between operations: 13.5 us -> 0.01 us
    unnamed x3 -> x0, waiting for transfers between devices: 145 us -> none
    psum x1 -> x0, blocking collectives: 121 us -> none  [body(): attn = lax.psum(partial_value, 'kv')]
    all_gather x3 -> x0, blocking collectives: 59.3 us -> none  [the longest x2 49.5 us: combined_all(): everything = jax.tree.map(lambda part: lax.all_gather(part, axis), x)]
    pallas_call x0 -> x1, Pallas kernels: none -> 49.9 us  [body(): pl.pallas_call(kernel, out_shape=jax.ShapeDtypeStruct((HERE, OUT_COLS), F...]
    add x65 -> x0, other arithmetic: 39.8 us -> none  [the longest x31 37.5 us: combine_parts(): weighted_a * factor_a[..., None] + weighted_b * factor_b[..., None]]
    dot_general x6 -> x0, matrix products: 24.1 us -> none  [the longest x1 7.19 us: body(): jnp.einsum('rhp,rpl->rhl', weights, latent_cache[:, :, :latent], preferre...]
    all_gather x1 -> x0, waiting for transfers between devices: 22.8 us -> none  [combined_all(): everything = jax.tree.map(lambda part: lax.all_gather(part, axis), x)]
  transfers between devices with their start and end apart: 2 -> 0, of which waited for: 2 -> 0; matrix products, arithmetic and copies ran while one was open for 1% -> 0% of each run, Pallas kernels for 0% -> 0%
where the time goes in v1:
time: 51.3 us; the launch traced here: 51.1 us
  Pallas kernels  49.9 us (97%)
  local copies, waits for them, and re-layouts  1.26 us (2%)
    pallas_call x1, Pallas kernels, body(): pl.pallas_call(kernel, out_shape=jax.ShapeDtypeStruct((HERE, OUT_COLS), F...  49.9 us
    unnamed x1, local copies, waits for them, and re-layouts  1.26 us

profile of v1, /device:TPU:1, one launch (start us, length us, event | category | flops | bytes accessed | tf_op | source)
XLA Modules:
  0.0 51.1 jit_solution(16190584987056128935)
XLA Ops:
  0.0 49.9 %shard_map.109 = f32[2,224]{1,0:T(2,128)} custom-call(bf16[2,576,128]{2,1,0:T(8,128)(2,1)} %bitcast.7, bf16[2,576,5120]{2,1,0:T(8,128)(2,1)} %bitcast.4, bf16[2,576]{1,0:T(2,128)(2,1)} %new_hbm.1, s32[2]{0:T(128)} %lengths_ref.1, bf16[4,512,128]{2,1,0:T(8,128)(2,1)} %uv_hbm.1, bf16[512,7168]{1,0:T(8,128)(2,1)} %wo_hbm.1, bf16[2,7168]{1,0:T(2,128)(2,1)} %hid_hbm.1, ...), custom_call_target="tpu_custom_call" | custom-call | tf_op jit(solution)/shard_map/pallas_call | solution.py:323
  49.9 1.3 %copy.13 = f32[2,224]{1,0:T(2,128)} copy(f32[2,224]{1,0:T(2,128)} %shard_map.109) | data formatting | bytes 3584

commit v2 on v1

--- a/solution.py
+++ b/solution.py
@@ -13,6 +13,7 @@
 KV, ROWS, HERE = 32, 4, 2
 OUT_COLS = D // KV
 CHUNK = 1024
+BLOCK = 256
 CHUNKS = SPAN // CHUNK
 REDUCERS = 14
 LOG2E = 1.4426950408889634
@@ -95,13 +96,10 @@
     sub = lax.broadcasted_iota(jnp.int32, (8, 128), 0)
     lane = lax.broadcasted_iota(jnp.int32, (8, 128), 1)
 
-    for copy in small:
-        copy.wait()
-    new_score = []
+    small[0].wait()
     for r in range(HERE):
-        q_f = qt[r].astype(F32).T
-        q[r] = q_f.astype(BF16)
-        new_score.append(jnp.sum(q_f * new[r : r + 1, :].astype(F32), axis=1, keepdims=True) * SCALE2)
+        q[r] = qt[r].astype(F32).T.astype(BF16)
+
     def packed(rows, j):
         base = 512 * j
         tile = rows[:, base : base + 128]
@@ -109,46 +107,59 @@
             tile = jnp.where(sub // 2 == c, rows[:, base + 128 * c : base + 128 * (c + 1)], tile)
         return tile
 
-    position = lax.broadcasted_iota(jnp.int32, (1, CHUNK), 1) + k * SPAN
+    position = lax.broadcasted_iota(jnp.int32, (1, BLOCK), 1) + k * SPAN
 
     def scores(r, c):
         cache[r][c].wait()
-        cols = pl.ds(c * CHUNK, CHUNK)
-        raw = dot(q[r], kt[r, :, cols]) * SCALE2
-        raw = jnp.where(position + c * CHUNK < lengths_ref[r], raw, NEG_FILL)
-        s[r, :, cols] = raw
-        return jnp.max(raw, axis=1, keepdims=True)
+        most = None
+        for first in range(c * CHUNK, (c + 1) * CHUNK, BLOCK):
+            cols = pl.ds(first, BLOCK)
+            raw = dot(q[r], kt[r, :, cols]) * SCALE2
+            raw = jnp.where(position + first < lengths_ref[r], raw, NEG_FILL)
+            s[r, :, cols] = raw
+            for part in range(0, BLOCK, 128):
+                piece = raw[:, part : part + 128]
+                most = piece if most is None else jnp.maximum(most, piece)
+        return most
 
     def weigh(r, c, top):
         cols = pl.ds(c * CHUNK, CHUNK)
         value = jnp.exp2(s[r, :, cols] - top)
         w[r, :, cols] = value.astype(BF16)
-        return jnp.sum(value, axis=1, keepdims=True)
-
-    def pv(r, c):
-        cols = pl.ds(c * CHUNK, CHUNK)
-        part = dot(w[r, :, cols], kt[r, :LATENT, cols], ((1,), (1,)))
-        if c == 0:
-            acc[r] = part
-        else:
-            acc[r] += part
-
-    top = list(new_score)
-    total = [jnp.zeros((HEADS, 1), F32)] * HERE
-    for c in range(CHUNKS):
-        top[0] = jnp.maximum(top[0], scores(0, c))
+        added = value[:, :128]
+        for part in range(128, CHUNK, 128):
+            added = added + value[:, part : part + 128]
+        return added
+
+    def highest(r, parts):
+        most = parts[0]
+        for part in parts[1:]:
+            most = jnp.maximum(most, part)
+        new_score = jnp.sum(q[r].astype(F32) * new[r : r + 1, :].astype(F32), axis=1, keepdims=True) * SCALE2
+        return new_score, jnp.maximum(jnp.max(most, axis=1, keepdims=True), new_score)
+
+    def summed(parts):
+        added = parts[0]
+        for part in parts[1:]:
+            added = added + part
+        return jnp.sum(added, axis=1, keepdims=True)
+
+    parts = [scores(0, c) for c in range(CHUNKS)]
+    small[1].wait()
+    new0, top0 = highest(0, parts)
     weights[0].start()
     weights[1].start()
+    parts, sums = [], []
     for c in range(CHUNKS):
-        top[1] = jnp.maximum(top[1], scores(1, c))
-        total[0] = total[0] + weigh(0, c, top[0])
+        parts.append(scores(1, c))
+        sums.append(weigh(0, c, top0))
     for copy in weights[2:]:
         copy.start()
-    for c in range(CHUNKS):
-        pv(0, c)
-        total[1] = total[1] + weigh(1, c, top[1])
-    for c in range(CHUNKS):
-        pv(1, c)
+    new1, top1 = highest(1, parts)
+    new_score, top = [new0, new1], [top0, top1]
+    total = [summed(sums), summed([weigh(1, c, top1) for c in range(CHUNKS)])]
+    for r in range(HERE):
+        acc[r] = dot(w[r], kt[r, :LATENT, :], ((1,), (1,)))
 
     half = lax.broadcasted_iota(jnp.int32, (16, 8, 128), 1) < 4
     left = lax.broadcasted_iota(jnp.int32, (HEADS, 128), 1) < 64
@@ -181,6 +192,8 @@
     send_kv(lambda peer: part_out.at[lax.div(peer, 2), lax.rem(peer, 2)], part_in.at[k], 1)
     part_in[k] = part_out[own_chip, own_core]
 
+    for copy in small[2:]:
+        copy.wait()
     hid_f = hid_in[...].astype(F32)
     hid_rows = jnp.where(lax.broadcasted_iota(jnp.int32, (8, D), 0) % 2 == 0, hid_f[0:1], hid_f[1:2])
 
@@ -294,8 +307,8 @@
     last_in[z] = mine
     send_row(last_own, last_in.at[z], 6)
     wait_for(recv_sem.at[6], last_in, ROWS - 1)
-    summed = jnp.sum(last_in[...], axis=0)
-    result = jnp.concatenate([summed[0:8], summed[8:16]], axis=1) + own_stream
+    final = jnp.sum(last_in[...], axis=0)
+    result = jnp.concatenate([final[0:8], final[8:16]], axis=1) + own_stream
     own = result[0:2]
     for zz in range(1, ROWS):
         own = jnp.where(z == zz, result[2 * zz : 2 * zz + 2], own)

time: 51.3 us -> 50 us (0.975)
  Pallas kernels: 49.9 us -> 48.6 us
    pallas_call x1, Pallas kernels: 49.9 us -> 48.6 us  [body(): pl.pallas_call(kernel, out_shape=jax.ShapeDtypeStruct((HERE, OUT_COLS), F...]
where the time goes in v2:
time: 50 us; the launch traced here: 49.8 us
  Pallas kernels  48.6 us (97%)
  local copies, waits for them, and re-layouts  1.26 us (3%)
    pallas_call x1, Pallas kernels, body(): pl.pallas_call(kernel, out_shape=jax.ShapeDtypeStruct((HERE, OUT_COLS), F...  48.6 us
    unnamed x1, local copies, waits for them, and re-layouts  1.26 us

profile of v2, /device:TPU:1, one launch (start us, length us, event | category | flops | bytes accessed | tf_op | source)
XLA Modules:
  0.0 49.8 jit_solution(7580424322376588280)
XLA Ops:
  0.0 48.6 %shard_map.109 = f32[2,224]{1,0:T(2,128)} custom-call(bf16[2,576,128]{2,1,0:T(8,128)(2,1)} %bitcast.7, bf16[2,576,5120]{2,1,0:T(8,128)(2,1)} %bitcast.4, bf16[2,576]{1,0:T(2,128)(2,1)} %new_hbm.1, s32[2]{0:T(128)} %lengths_ref.1, bf16[4,512,128]{2,1,0:T(8,128)(2,1)} %uv_hbm.1, bf16[512,7168]{1,0:T(8,128)(2,1)} %wo_hbm.1, bf16[2,7168]{1,0:T(2,128)(2,1)} %hid_hbm.1, ...), custom_call_target="tpu_custom_call" | custom-call | tf_op jit(solution)/shard_map/pallas_call | solution.py:336
  48.6 1.3 %copy.13 = f32[2,224]{1,0:T(2,128)} copy(f32[2,224]{1,0:T(2,128)} %shard_map.109) | data formatting | bytes 3584

commit v3 on v2

--- a/solution.py
+++ b/solution.py
@@ -71,8 +71,13 @@
     chips = [xs[dx] + ys[dy] for dx, dy in offsets]
     peers = [2 * chip + core for chip in chips for core in cores]
     del peers[-2]
-    row_peers = [lax.rem(z + d, ROWS) * KV + k for d in (2, 1, 3)]
-    for peer in [plane + p for p in peers] + row_peers:
+    zs = [KV * lax.rem(z + d, ROWS) for d in range(ROWS)]
+    row_peers = [zs[d] + k for d in (2, 1, 3)]
+    near = [(lax.div(xs[dx], 4) * 2 + core, plane + 2 * (xs[dx] + ys[0]) + core) for dx in (2, 1, 3, 0) for core in cores]
+    del near[-2]
+    far = sorted(((dz, dy) for dz in range(ROWS) for dy in range(4)), key=lambda o: -min(o[0], 4 - o[0]) - min(o[1], 4 - o[1]))
+    far = [(ys[dy], zs[dz] + 2 * (xs[0] + ys[dy]) + own_core, dz, dy) for dz, dy in far[:-1]]
+    for peer in [plane + p for p in peers] + [device for _, device, dz, _ in far if dz]:
         pl.semaphore_signal(barrier, inc=1, device_id=peer, device_id_type=LOGICAL)
 
     def send(src, dst, lane, device):
@@ -188,7 +193,7 @@
             part_out[:, core, r] = jnp.concatenate([both[0][core], both[1][core]], axis=1).astype(BF16)
     for core in range(2):
         part_out[:, core, HERE] = jnp.concatenate([logs[0][core], logs[1][core]], axis=1).astype(BF16)
-    pl.semaphore_wait(barrier, KV - 1 + ROWS - 1)
+    pl.semaphore_wait(barrier, KV - 1 + 12)
     send_kv(lambda peer: part_out.at[lax.div(peer, 2), lax.rem(peer, 2)], part_in.at[k], 1)
     part_in[k] = part_out[own_chip, own_core]
 
@@ -273,13 +278,20 @@
     stream = jnp.concatenate(
         [parts[t // 4, (t // 2) % 2, 8 * (t % 2) : 8 * (t % 2) + 8] for t in range(D // 128)], axis=1
     )
-    mean_sq = jnp.sum(stream * stream, axis=1, keepdims=True) * (1.0 / D)
-    normed = (stream * lax.rsqrt(mean_sq + 1e-06) * gain[...].astype(F32).reshape(1, D)).astype(BF16)
+    scaled = (stream * gain[...].astype(F32).reshape(1, D)).astype(BF16)
     for copy in weights[2:4]:
         copy.wait()
-    gate_proj = dot(normed, wg[...], ((1,), (1,)))
-    up_proj = dot(normed, wu[...], ((1,), (1,)))
-    hidden = (gate_proj / (1.0 + jnp.exp(-gate_proj)) * up_proj).astype(BF16)
+
+    def project(weight):
+        parts = [
+            dot(scaled[:, first : first + 3584], weight[:, first : first + 3584], ((1,), (1,))) for first in (0, 3584)
+        ]
+        return parts[0] + parts[1]
+
+    gate_proj, up_proj = project(wg), project(wu)
+    rstd = lax.rsqrt(jnp.sum(stream * stream, axis=1, keepdims=True) * (1.0 / D) + 1e-06)
+    gate_proj = gate_proj * rstd
+    hidden = (gate_proj / (1.0 + jnp.exp(-gate_proj)) * (up_proj * rstd)).astype(BF16)
     weights[4].wait()
     down = dot(hidden, wd[...])
     down = jnp.concatenate([down, jnp.zeros((8, 128), F32)], axis=1)
@@ -291,9 +303,11 @@
             two = [jnp.where(lane < 128 - shift, turned[i], turned[i + 1]) for i in range(2)]
         else:
             two = three[:2]
-        down_out[p] = jnp.concatenate(two, axis=0).astype(BF16)
-    down_in[k] = down_out[k]
-    send_kv(lambda peer: down_out.at[peer], down_in.at[k], 5)
+        down_out[p // 8 * 2 + p % 2, p // 2 % 4] = jnp.concatenate(two, axis=0).astype(BF16)
+    own_near = lax.div(xs[0], 4) * 2 + own_core
+    for block, device in near:
+        send(down_out.at[block], down_in.at[own_near], 5, device)
+    down_in[own_near] = down_out[own_near]
 
     own_tile = lax.div(7 * k, 4)
     wide_stream[:, pl.ds(0, D)] = stream
@@ -301,22 +315,22 @@
     own_stream = wide_stream[:, pl.ds(pl.multiple_of(own_tile * 128, 128), 512)]
     own_stream = pltpu.roll(own_stream, lax.rem(512 - (OUT_COLS * k - 128 * own_tile), 512), 1)[:, :256]
 
-    wait_for(recv_sem.at[5], down_in, KV - 1)
-    mine = jnp.sum(down_in[...].astype(F32), axis=0)
-    last_own[...] = mine
-    last_in[z] = mine
-    send_row(last_own, last_in.at[z], 6)
-    wait_for(recv_sem.at[6], last_in, ROWS - 1)
-    final = jnp.sum(last_in[...], axis=0)
+    wait_for(recv_sem.at[5], down_in, 7)
+    last_own[...] = jnp.sum(down_in[...].astype(F32), axis=0).astype(BF16)
+    own_far = 4 * z + ys[0]
+    for y, device, _, _ in far:
+        send(last_own.at[y], last_in.at[own_far], 6, device)
+    last_in[own_far] = last_own[ys[0]]
+    wait_for(recv_sem.at[6], last_in, 15)
+    final = jnp.sum(last_in[...].astype(F32), axis=0)
     result = jnp.concatenate([final[0:8], final[8:16]], axis=1) + own_stream
     own = result[0:2]
     for zz in range(1, ROWS):
         own = jnp.where(z == zz, result[2 * zz : 2 * zz + 2], own)
     out_ref[...] = own[:, :OUT_COLS]
 
-    for i, buffer in ((1, part_in), (5, down_in)):
-        wait_for(send_sem.at[i], buffer, KV - 1)
-    wait_for(send_sem.at[6], last_in, ROWS - 1)
+    for i, buffer, count in ((1, part_in, KV - 1), (5, down_in, 7), (6, last_in, 15)):
+        wait_for(send_sem.at[i], buffer, count)
 
     @pl.when(reducer)
     def _():
@@ -362,10 +376,10 @@
             vmem((8, 128), F32),
             vmem((REDUCERS, 2, 16, 128), BF16),
             vmem((2, 16, 128), BF16),
-            vmem((KV, 16, 128), BF16),
-            vmem((KV, 16, 128), BF16),
-            vmem((16, 128), F32),
-            vmem((ROWS, 16, 128), F32),
+            vmem((8, 4, 16, 128), BF16),
+            vmem((8, 4, 16, 128), BF16),
+            vmem((4, 16, 128), BF16),
+            vmem((16, 16, 128), BF16),
             vmem((8, D + 512), F32),
             pltpu.SemaphoreType.DMA((9,)),
             pltpu.SemaphoreType.DMA((HERE, CHUNKS)),

time: 50 us -> 50.3 us (level)
  no operation moved by 1% of the time
where the time goes in v3:
time: 50.3 us; the launch traced here: 50.2 us
  Pallas kernels  48.9 us (97%)
  local copies, waits for them, and re-layouts  1.26 us (3%)
    pallas_call x1, Pallas kernels, body(): pl.pallas_call(kernel, out_shape=jax.ShapeDtypeStruct((HERE, OUT_COLS), F...  48.9 us
    unnamed x1, local copies, waits for them, and re-layouts  1.26 us

profile of v3, /device:TPU:1, one launch (start us, length us, event | category | flops | bytes accessed | tf_op | source)
XLA Modules:
  0.0 50.2 jit_solution(15041419809235271050)
XLA Ops:
  0.0 48.9 %shard_map.109 = f32[2,224]{1,0:T(2,128)} custom-call(bf16[2,576,128]{2,1,0:T(8,128)(2,1)} %bitcast.7, bf16[2,576,5120]{2,1,0:T(8,128)(2,1)} %bitcast.4, bf16[2,576]{1,0:T(2,128)(2,1)} %new_hbm.1, s32[2]{0:T(128)} %lengths_ref.1, bf16[4,512,128]{2,1,0:T(8,128)(2,1)} %uv_hbm.1, bf16[512,7168]{1,0:T(8,128)(2,1)} %wo_hbm.1, bf16[2,7168]{1,0:T(2,128)(2,1)} %hid_hbm.1, ...), custom_call_target="tpu_custom_call" | custom-call | tf_op jit(solution)/shard_map/pallas_call | solution.py:350
  48.9 1.3 %copy.13 = f32[2,224]{1,0:T(2,128)} copy(f32[2,224]{1,0:T(2,128)} %shard_map.109) | data formatting | bytes 3584

commit v4 on v2

--- a/solution.py
+++ b/solution.py
@@ -159,7 +159,7 @@
     new_score, top = [new0, new1], [top0, top1]
     total = [summed(sums), summed([weigh(1, c, top1) for c in range(CHUNKS)])]
     for r in range(HERE):
-        acc[r] = dot(w[r], kt[r, :LATENT, :], ((1,), (1,)))
+        acc[r] = dot(kt[r, :LATENT, :], w[r], ((1,), (1,)))
 
     half = lax.broadcasted_iota(jnp.int32, (16, 8, 128), 1) < 4
     left = lax.broadcasted_iota(jnp.int32, (HEADS, 128), 1) < 64
@@ -181,7 +181,7 @@
         middle = rounded(log_total - high)
         low = log_total - high - middle
         logs.append(share(jnp.where(left, high, middle), jnp.where(left, low, wide_zero)))
-        mine = (acc[r] + own_new * new[r : r + 1, :LATENT].astype(F32)) * (1.0 / norm)
+        mine = (acc[r].T + own_new * new[r : r + 1, :LATENT].astype(F32)) * (1.0 / norm)
         quarters = [mine[:, 128 * c : 128 * c + 128] for c in range(4)]
         both = [share(quarters[2 * u], quarters[2 * u + 1]) for u in range(2)]
         for core in range(2):
@@ -352,7 +352,7 @@
             vmem((HERE, HEADS, QK), BF16),
             vmem((HERE, HEADS, SPAN), F32),
             vmem((HERE, HEADS, SPAN), BF16),
-            vmem((HERE, HEADS, LATENT), F32),
+            vmem((HERE, LATENT, HEADS), F32),
             vmem((REDUCERS, 8, 128), F32),
             vmem((KV // 2, 2, HERE + 1, 16, 128), BF16),
             vmem((KV, HERE + 1, 16, 128), BF16),

time: 50 us -> 49.5 us (0.990)
  Pallas kernels: 48.6 us -> 48.1 us
where the time goes in v4:
time: 49.5 us; the launch traced here: 49.4 us
  Pallas kernels  48.1 us (97%)
  local copies, waits for them, and re-layouts  1.26 us (3%)
    pallas_call x1, Pallas kernels, body(): pl.pallas_call(kernel, out_shape=jax.ShapeDtypeStruct((HERE, OUT_COLS), F...  48.1 us
    unnamed x1, local copies, waits for them, and re-layouts  1.26 us

profile of v4, /device:TPU:1, one launch (start us, length us, event | category | flops | bytes accessed | tf_op | source)
XLA Modules:
  0.0 49.4 jit_solution(134538014560679047)
XLA Ops:
  0.0 48.1 %shard_map.109 = f32[2,224]{1,0:T(2,128)} custom-call(bf16[2,576,128]{2,1,0:T(8,128)(2,1)} %bitcast.7, bf16[2,576,5120]{2,1,0:T(8,128)(2,1)} %bitcast.4, bf16[2,576]{1,0:T(2,128)(2,1)} %new_hbm.1, s32[2]{0:T(128)} %lengths_ref.1, bf16[4,512,128]{2,1,0:T(8,128)(2,1)} %uv_hbm.1, bf16[512,7168]{1,0:T(8,128)(2,1)} %wo_hbm.1, bf16[2,7168]{1,0:T(2,128)(2,1)} %hid_hbm.1, ...), custom_call_target="tpu_custom_call" | custom-call | tf_op jit(solution)/shard_map/pallas_call | solution.py:336
  48.1 1.3 %copy.13 = f32[2,224]{1,0:T(2,128)} copy(f32[2,224]{1,0:T(2,128)} %shard_map.109) | data formatting | bytes 3584

commit v5 on v4

--- a/solution.py
+++ b/solution.py
@@ -12,9 +12,9 @@
 D, LOCAL_FF, SPAN = 7168, 144, 5120
 KV, ROWS, HERE = 32, 4, 2
 OUT_COLS = D // KV
-CHUNK = 1024
+PIECES = ((0, 1024, 3072, SPAN), (0, 2560, SPAN))
 BLOCK = 256
-CHUNKS = SPAN // CHUNK
+BLOCKS = SPAN // BLOCK
 REDUCERS = 14
 LOG2E = 1.4426950408889634
 SCALE2 = LOG2E * (HEAD_DIM + ROPE) ** -0.5
@@ -43,18 +43,14 @@
     ]
     for copy in small:
         copy.start()
-    cache = [
-        [
-            pltpu.make_async_copy(
-                cache_hbm.at[r, :, pl.ds(c * CHUNK, CHUNK)], kt.at[r, :, pl.ds(c * CHUNK, CHUNK)], cache_sem.at[r, c]
-            )
-            for c in range(CHUNKS)
-        ]
-        for r in range(HERE)
-    ]
+    cache = []
     for r in range(HERE):
-        for c in range(CHUNKS):
-            cache[r][c].start()
+        for c, (first, end) in enumerate(zip(PIECES[r], PIECES[r][1:])):
+            span = pl.ds(first, end - first)
+            copy = pltpu.make_async_copy(cache_hbm.at[r, :, span], kt.at[r, :, span], cache_sem.at[r, c])
+            copy.start()
+            cache.append((r, first, copy))
+
     weights = [
         pltpu.make_async_copy(src, dst, in_sem.at[4 + i])
         for i, (src, dst) in enumerate(((uv_hbm, uv), (wo_hbm, wo), (gate_hbm, wg), (up_hbm, wu), (down_hbm, wd)))
@@ -109,57 +105,55 @@
 
     position = lax.broadcasted_iota(jnp.int32, (1, BLOCK), 1) + k * SPAN
 
-    def scores(r, c):
-        cache[r][c].wait()
-        most = None
-        for first in range(c * CHUNK, (c + 1) * CHUNK, BLOCK):
-            cols = pl.ds(first, BLOCK)
-            raw = dot(q[r], kt[r, :, cols]) * SCALE2
-            raw = jnp.where(position + first < lengths_ref[r], raw, NEG_FILL)
-            s[r, :, cols] = raw
-            for part in range(0, BLOCK, 128):
-                piece = raw[:, part : part + 128]
-                most = piece if most is None else jnp.maximum(most, piece)
-        return most
-
-    def weigh(r, c, top):
-        cols = pl.ds(c * CHUNK, CHUNK)
+    def largest(value, so_far):
+        for part in range(0, BLOCK, 128):
+            piece = value[:, part : part + 128]
+            so_far = piece if so_far is None else jnp.maximum(so_far, piece)
+        return so_far
+
+    def scores(r, i, so_far):
+        for row, first, copy in cache:
+            if (row, first) == (r, BLOCK * i):
+                copy.wait()
+        cols = pl.ds(BLOCK * i, BLOCK)
+        raw = dot(q[r], kt[r, :, cols]) * SCALE2
+        raw = jnp.where(position + BLOCK * i < lengths_ref[r], raw, NEG_FILL)
+        s[r, :, cols] = raw
+        return largest(raw, so_far)
+
+    def weigh(r, i, top, so_far):
+        cols = pl.ds(BLOCK * i, BLOCK)
         value = jnp.exp2(s[r, :, cols] - top)
         w[r, :, cols] = value.astype(BF16)
-        added = value[:, :128]
-        for part in range(128, CHUNK, 128):
-            added = added + value[:, part : part + 128]
-        return added
-
-    def highest(r, parts):
-        most = parts[0]
-        for part in parts[1:]:
-            most = jnp.maximum(most, part)
+        for part in range(0, BLOCK, 128):
+            piece = value[:, part : part + 128]
+            so_far = piece if so_far is None else so_far + piece
+        return so_far
+
+    def highest(r, most):
         new_score = jnp.sum(q[r].astype(F32) * new[r : r + 1, :].astype(F32), axis=1, keepdims=True) * SCALE2
         return new_score, jnp.maximum(jnp.max(most, axis=1, keepdims=True), new_score)
 
-    def summed(parts):
-        added = parts[0]
-        for part in parts[1:]:
-            added = added + part
-        return jnp.sum(added, axis=1, keepdims=True)
-
-    parts = [scores(0, c) for c in range(CHUNKS)]
+    most0 = None
+    for i in range(BLOCKS):
+        most0 = scores(0, i, most0)
     small[1].wait()
-    new0, top0 = highest(0, parts)
-    weights[0].start()
-    weights[1].start()
-    parts, sums = [], []
-    for c in range(CHUNKS):
-        parts.append(scores(1, c))
-        sums.append(weigh(0, c, top0))
-    for copy in weights[2:]:
+    new0, top0 = highest(0, most0)
+    most1 = sum0 = sum1 = None
+    for i in range(BLOCKS):
+        most1 = scores(1, i, most1)
+        sum0 = weigh(0, i, top0, sum0)
+    for copy in weights:
         copy.start()
-    new1, top1 = highest(1, parts)
+    new1, top1 = highest(1, most1)
+    for half in range(2):
+        rows = slice(256 * half, 256 * half + 256)
+        acc[0, rows] = dot(kt[0, rows, :], w[0], ((1,), (1,)))
+        for i in range(BLOCKS // 2 * half, BLOCKS // 2 * (half + 1)):
+            sum1 = weigh(1, i, top1, sum1)
+    acc[1] = dot(kt[1, :LATENT, :], w[1], ((1,), (1,)))
     new_score, top = [new0, new1], [top0, top1]
-    total = [summed(sums), summed([weigh(1, c, top1) for c in range(CHUNKS)])]
-    for r in range(HERE):
-        acc[r] = dot(kt[r, :LATENT, :], w[r], ((1,), (1,)))
+    total = [jnp.sum(value, axis=1, keepdims=True) for value in (sum0, sum1)]
 
     half = lax.broadcasted_iota(jnp.int32, (16, 8, 128), 1) < 4
     left = lax.broadcasted_iota(jnp.int32, (HEADS, 128), 1) < 64
@@ -368,7 +362,7 @@
             vmem((ROWS, 16, 128), F32),
             vmem((8, D + 512), F32),
             pltpu.SemaphoreType.DMA((9,)),
-            pltpu.SemaphoreType.DMA((HERE, CHUNKS)),
+            pltpu.SemaphoreType.DMA((HERE, 3)),
             pltpu.SemaphoreType.DMA((7,)),
             pltpu.SemaphoreType.DMA((7,)),
         ],

time: 49.5 us -> 49.9 us (level)
  no operation moved by 1% of the time
where the time goes in v5:
time: 49.9 us; the launch traced here: 49.8 us
  Pallas kernels  48.5 us (97%)
  local copies, waits for them, and re-layouts  1.26 us (3%)
    pallas_call x1, Pallas kernels, body(): pl.pallas_call(kernel, out_shape=jax.ShapeDtypeStruct((HERE, OUT_COLS), F...  48.5 us
    unnamed x1, local copies, waits for them, and re-layouts  1.26 us

profile of v5, /device:TPU:1, one launch (start us, length us, event | category | flops | bytes accessed | tf_op | source)
XLA Modules:
  0.0 49.8 jit_solution(16017673294448775410)
XLA Ops:
  0.0 48.5 %shard_map.109 = f32[2,224]{1,0:T(2,128)} custom-call(bf16[2,576,128]{2,1,0:T(8,128)(2,1)} %bitcast.7, bf16[2,576,5120]{2,1,0:T(8,128)(2,1)} %bitcast.4, bf16[2,576]{1,0:T(2,128)(2,1)} %new_hbm.1, s32[2]{0:T(128)} %lengths_ref.1, bf16[4,512,128]{2,1,0:T(8,128)(2,1)} %uv_hbm.1, bf16[512,7168]{1,0:T(8,128)(2,1)} %wo_hbm.1, bf16[2,7168]{1,0:T(2,128)(2,1)} %hid_hbm.1, ...), custom_call_target="tpu_custom_call" | custom-call | tf_op jit(solution)/shard_map/pallas_call | solution.py:330
  48.5 1.3 %copy.13 = f32[2,224]{1,0:T(2,128)} copy(f32[2,224]{1,0:T(2,128)} %shard_map.109) | data formatting | bytes 3584

commit v6 on v4

--- a/solution.py
+++ b/solution.py
@@ -29,8 +29,8 @@
     q_hbm, cache_hbm, new_hbm, lengths_ref, uv_hbm, wo_hbm, hid_hbm, gain_hbm, gate_hbm, up_hbm, down_hbm,
     out_ref,
     qt, kt, new, uv, wo, hid_in, gain, wg, wu, wd,
-    q, s, w, acc, hid_tiles,
-    part_out, part_in, attn_out, attn_in, row_tiles, stream_own, stream_all, wide,
+    q, s, w, hid_tiles,
+    log_out, log_in, part_out, part_in, attn_out, attn_in, row_tiles, stream_own, stream_all, wide,
     down_out, down_in, last_own, last_in, wide_stream,
     in_sem, cache_sem, send_sem, recv_sem,
 ):
@@ -158,9 +158,6 @@
     new1, top1 = highest(1, parts)
     new_score, top = [new0, new1], [top0, top1]
     total = [summed(sums), summed([weigh(1, c, top1) for c in range(CHUNKS)])]
-    for r in range(HERE):
-        acc[r] = dot(kt[r, :LATENT, :], w[r], ((1,), (1,)))
-
     half = lax.broadcasted_iota(jnp.int32, (16, 8, 128), 1) < 4
     left = lax.broadcasted_iota(jnp.int32, (HEADS, 128), 1) < 64
     wide_zero = jnp.zeros((HEADS, 128), F32)
@@ -172,7 +169,7 @@
     def rounded(value):
         return value.astype(BF16).astype(F32)
 
-    logs = []
+    logs, norms, own_news = [], [], []
     for r in range(HERE):
         own_new = jnp.where(k == 0, jnp.exp2(new_score[r] - top[r]), 0.0)
         norm = jnp.maximum(total[r] + own_new, 1e-30)
@@ -181,16 +178,23 @@
         middle = rounded(log_total - high)
         low = log_total - high - middle
         logs.append(share(jnp.where(left, high, middle), jnp.where(left, low, wide_zero)))
-        mine = (acc[r].T + own_new * new[r : r + 1, :LATENT].astype(F32)) * (1.0 / norm)
+        norms.append(norm)
+        own_news.append(own_new)
+    for core in range(2):
+        log_out[:, core] = jnp.concatenate([logs[0][core], logs[1][core]], axis=1).astype(BF16)
+    pl.semaphore_wait(barrier, KV - 1 + ROWS - 1)
+    send_kv(lambda peer: log_out.at[lax.div(peer, 2), lax.rem(peer, 2)], log_in.at[k], 0)
+    log_in[k] = log_out[own_chip, own_core]
+
+    for r in range(HERE):
+        value = dot(kt[r, :LATENT, :], w[r], ((1,), (1,))).T
+        mine = (value + own_news[r] * new[r : r + 1, :LATENT].astype(F32)) * (1.0 / norms[r])
         quarters = [mine[:, 128 * c : 128 * c + 128] for c in range(4)]
         both = [share(quarters[2 * u], quarters[2 * u + 1]) for u in range(2)]
         for core in range(2):
-            part_out[:, core, r] = jnp.concatenate([both[0][core], both[1][core]], axis=1).astype(BF16)
-    for core in range(2):
-        part_out[:, core, HERE] = jnp.concatenate([logs[0][core], logs[1][core]], axis=1).astype(BF16)
-    pl.semaphore_wait(barrier, KV - 1 + ROWS - 1)
-    send_kv(lambda peer: part_out.at[lax.div(peer, 2), lax.rem(peer, 2)], part_in.at[k], 1)
-    part_in[k] = part_out[own_chip, own_core]
+            part_out[r, :, core] = jnp.concatenate([both[0][core], both[1][core]], axis=1).astype(BF16)
+        send_kv(lambda peer: part_out.at[r, lax.div(peer, 2), lax.rem(peer, 2)], part_in.at[r, k], 1 + 6 * r)
+        part_in[r, k] = part_out[r, own_chip, own_core]
 
     for copy in small[2:]:
         copy.wait()
@@ -200,16 +204,17 @@
     for j in range(REDUCERS):
         hid_tiles[j] = packed(hid_rows, j)
 
-    wait_for(recv_sem.at[1], part_in, KV - 1)
     weights[0].wait()
+    wait_for(recv_sem.at[0], log_in, KV - 1)
     att = []
     for r in range(HERE):
-        log_parts = part_in[:, HERE, 8 * r : 8 * r + 8].astype(F32)
+        log_parts = log_in[:, 8 * r : 8 * r + 8].astype(F32)
         log_parts = log_parts + pltpu.roll(log_parts, 64, 2)
         log_parts = log_parts + pltpu.roll(log_parts, 4, 1)
         factor = jnp.exp2(log_parts - jnp.max(log_parts, axis=0)[None])
         factor = factor * (1.0 / jnp.sum(factor, axis=0))[None]
-        data = part_in[:, r].astype(F32)
+        wait_for(recv_sem.at[1 + 6 * r], part_in.at[r], KV - 1)
+        data = part_in[r].astype(F32)
         att.append([jnp.sum(data[:, 8 * u : 8 * u + 8] * factor, axis=0) for u in range(2)])
     pieces = []
     for c in range(4):
@@ -314,7 +319,7 @@
         own = jnp.where(z == zz, result[2 * zz : 2 * zz + 2], own)
     out_ref[...] = own[:, :OUT_COLS]
 
-    for i, buffer in ((1, part_in), (5, down_in)):
+    for i, buffer in ((0, log_in), (1, part_in.at[0]), (7, part_in.at[1]), (5, down_in)):
         wait_for(send_sem.at[i], buffer, KV - 1)
     wait_for(send_sem.at[6], last_in, ROWS - 1)
 
@@ -352,10 +357,11 @@
             vmem((HERE, HEADS, QK), BF16),
             vmem((HERE, HEADS, SPAN), F32),
             vmem((HERE, HEADS, SPAN), BF16),
-            vmem((HERE, LATENT, HEADS), F32),
             vmem((REDUCERS, 8, 128), F32),
-            vmem((KV // 2, 2, HERE + 1, 16, 128), BF16),
-            vmem((KV, HERE + 1, 16, 128), BF16),
+            vmem((KV // 2, 2, 16, 128), BF16),
+            vmem((KV, 16, 128), BF16),
+            vmem((HERE, KV // 2, 2, 16, 128), BF16),
+            vmem((HERE, KV, 16, 128), BF16),
             vmem((REDUCERS, 8, 128), F32),
             vmem((KV, 8, 128), F32),
             vmem((ROWS, 8, 128), F32),
@@ -369,8 +375,8 @@
             vmem((8, D + 512), F32),
             pltpu.SemaphoreType.DMA((9,)),
             pltpu.SemaphoreType.DMA((HERE, CHUNKS)),
-            pltpu.SemaphoreType.DMA((7,)),
-            pltpu.SemaphoreType.DMA((7,)),
+            pltpu.SemaphoreType.DMA((8,)),
+            pltpu.SemaphoreType.DMA((8,)),
         ],
         compiler_params=pltpu.CompilerParams(
             collective_id=0, has_side_effects=True, vmem_limit_bytes=60 * 1024 * 1024

time: 49.5 us -> 50.6 us (1.022)
  Pallas kernels: 48.1 us -> 49.2 us
    pallas_call x1, Pallas kernels: 48.1 us -> 49.2 us  [body(): pl.pallas_call(kernel, out_shape=jax.ShapeDtypeStruct((HERE, OUT_COLS), F...]
where the time goes in v6:
time: 50.6 us; the launch traced here: 50.5 us
  Pallas kernels  49.2 us (97%)
  local copies, waits for them, and re-layouts  1.26 us (2%)
    pallas_call x1, Pallas kernels, body(): pl.pallas_call(kernel, out_shape=jax.ShapeDtypeStruct((HERE, OUT_COLS), F...  49.2 us
    unnamed x1, local copies, waits for them, and re-layouts  1.26 us

profile of v6, /device:TPU:1, one launch (start us, length us, event | category | flops | bytes accessed | tf_op | source)
XLA Modules:
  0.0 50.5 jit_solution(14152983639970769708)
XLA Ops:
  0.0 49.2 %shard_map.109 = f32[2,224]{1,0:T(2,128)} custom-call(bf16[2,576,128]{2,1,0:T(8,128)(2,1)} %bitcast.7, bf16[2,576,5120]{2,1,0:T(8,128)(2,1)} %bitcast.4, bf16[2,576]{1,0:T(2,128)(2,1)} %new_hbm.1, s32[2]{0:T(128)} %lengths_ref.1, bf16[4,512,128]{2,1,0:T(8,128)(2,1)} %uv_hbm.1, bf16[512,7168]{1,0:T(8,128)(2,1)} %wo_hbm.1, bf16[2,7168]{1,0:T(2,128)(2,1)} %hid_hbm.1, ...), custom_call_target="tpu_custom_call" | custom-call | tf_op jit(solution)/shard_map/pallas_call | solution.py:341
  49.2 1.3 %copy.13 = f32[2,224]{1,0:T(2,128)} copy(f32[2,224]{1,0:T(2,128)} %shard_map.109) | data formatting | bytes 3584

commit v7 on v4

--- a/solution.py
+++ b/solution.py
@@ -32,7 +32,7 @@
     q, s, w, acc, hid_tiles,
     part_out, part_in, attn_out, attn_in, row_tiles, stream_own, stream_all, wide,
     down_out, down_in, last_own, last_in, wide_stream,
-    in_sem, cache_sem, send_sem, recv_sem,
+    in_sem, cache_sem, send_sem, recv_sem, stream_sem,
 ):
     k = lax.axis_index("kv")
     z = lax.axis_index("row")
@@ -225,15 +225,15 @@
         values.append(jnp.where(sub % 2 == 0, got[h : h + 1], got[4 + h : 5 + h]))
     head_values = jnp.concatenate(values, axis=1).astype(BF16)
     weights[1].wait()
-    partial = dot(head_values, wo[...])
-    for j in range(REDUCERS):
-        attn_out[j] = packed(partial, j)
-
-    for chip in chips:
-
-        @pl.when(jnp.logical_and(chip < REDUCERS, k != 2 * chip))
-        def _(chip=chip):
-            send(attn_out.at[chip], attn_in.at[k], 2, plane + 2 * chip)
+    for low in (0, 7):
+        partial = dot(head_values, wo[:, 512 * low : 512 * (low + 7)])
+        for j in range(7):
+            attn_out[low + j] = packed(partial, j)
+        for chip in chips:
+
+            @pl.when(jnp.logical_and(jnp.logical_and(chip >= low, chip < low + 7), k != 2 * chip))
+            def _(chip=chip):
+                send(attn_out.at[chip], attn_in.at[k], 2, plane + 2 * chip)
 
     reducer = jnp.logical_and(k % 2 == 0, k < 2 * REDUCERS)
 
@@ -262,41 +262,62 @@
             both = jnp.concatenate(tiles[2 * u : 2 * u + 2], axis=0).astype(BF16)
             wide[u] = both
             stream_all[j, u] = both
-        send_kv(lambda peer: wide, stream_all.at[j], 4)
-        wait_for(recv_sem.at[4], stream_all, REDUCERS - 1)
-
-    @pl.when(jnp.logical_not(reducer))
-    def _():
-        wait_for(recv_sem.at[4], stream_all, REDUCERS)
-
-    parts = stream_all[...].astype(F32)
-    stream = jnp.concatenate(
-        [parts[t // 4, (t // 2) % 2, 8 * (t % 2) : 8 * (t % 2) + 8] for t in range(D // 128)], axis=1
-    )
-    mean_sq = jnp.sum(stream * stream, axis=1, keepdims=True) * (1.0 / D)
-    normed = (stream * lax.rsqrt(mean_sq + 1e-06) * gain[...].astype(F32).reshape(1, D)).astype(BF16)
+        late = jnp.where(j < 7, 0, 1)
+        for peer in peers:
+            pltpu.make_async_remote_copy(
+                src_ref=wide, dst_ref=stream_all.at[j], send_sem=send_sem.at[4], recv_sem=stream_sem.at[late],
+                device_id=plane + peer, device_id_type=LOGICAL,
+            ).start()
+
     for copy in weights[2:4]:
         copy.wait()
-    gate_proj = dot(normed, wg[...], ((1,), (1,)))
-    up_proj = dot(normed, wu[...], ((1,), (1,)))
-    hidden = (gate_proj / (1.0 + jnp.exp(-gate_proj)) * up_proj).astype(BF16)
+    squares = jnp.zeros((8, 128), F32)
+    gate_proj = up_proj = jnp.zeros((8, LOCAL_FF), F32)
+    for g in range(2):
+        low = 7 * g
+        owner = jnp.logical_and(reducer, jnp.logical_and(own_chip >= low, own_chip < low + 7))
+
+        @pl.when(owner)
+        def _():
+            wait_for(stream_sem.at[g], stream_all, 6)
+
+        @pl.when(jnp.logical_not(owner))
+        def _():
+            wait_for(stream_sem.at[g], stream_all, 7)
+
+        parts = stream_all[low : low + 7].astype(F32)
+        tiles = [parts[t // 4, (t // 2) % 2, 8 * (t % 2) : 8 * (t % 2) + 8] for t in range(28)]
+        for tile in tiles:
+            squares = squares + tile * tile
+        cols = pl.ds(3584 * g, 3584)
+        stream = jnp.concatenate(tiles, axis=1)
+        wide_stream[:, cols] = stream
+        scaled = (stream * gain[cols].astype(F32).reshape(1, 3584)).astype(BF16)
+        gate_proj = gate_proj + dot(scaled, wg[:, cols], ((1,), (1,)))
+        up_proj = up_proj + dot(scaled, wu[:, cols], ((1,), (1,)))
+    rstd = lax.rsqrt(jnp.sum(squares, axis=1, keepdims=True) * (1.0 / D) + 1e-06)
+    gate_proj = gate_proj * rstd
+    hidden = (gate_proj / (1.0 + jnp.exp(-gate_proj)) * (up_proj * rstd)).astype(BF16)
     weights[4].wait()
-    down = dot(hidden, wd[...])
-    down = jnp.concatenate([down, jnp.zeros((8, 128), F32)], axis=1)
-    for p in range(KV):
-        tile, shift = divmod(OUT_COLS * p, 128)
-        three = [down[:, 128 * (tile + i) : 128 * (tile + i + 1)] for i in range(3)]
-        if shift:
-            turned = [pltpu.roll(t, 128 - shift, 1) for t in three]
-            two = [jnp.where(lane < 128 - shift, turned[i], turned[i + 1]) for i in range(2)]
-        else:
-            two = three[:2]
-        down_out[p] = jnp.concatenate(two, axis=0).astype(BF16)
+    own_half, in_half = lax.div(k, 16), lax.rem(k, 16)
+    for own, first in enumerate((16 - 16 * own_half, 16 * own_half)):
+        down = dot(hidden, wd[:, pl.ds(pl.multiple_of(first * OUT_COLS, 128), 3584)])
+        down = jnp.concatenate([down, jnp.zeros((8, 128), F32)], axis=1)
+        for p in range(16):
+            tile, shift = divmod(OUT_COLS * p, 128)
+            three = [down[:, 128 * (tile + i) : 128 * (tile + i + 1)] for i in range(3 if shift else 2)]
+            if shift:
+                turned = [pltpu.roll(t, 128 - shift, 1) for t in three]
+                two = [jnp.where(lane < 128 - shift, turned[i], turned[i + 1]) for i in range(2)]
+            else:
+                two = three
+            down_out[first + p] = jnp.concatenate(two, axis=0).astype(BF16)
+        for d in range(own, 16):
+            peer = first + lax.rem(in_half + d, 16)
+            send(down_out.at[peer], down_in.at[k], 5, plane + peer)
     down_in[k] = down_out[k]
-    send_kv(lambda peer: down_out.at[peer], down_in.at[k], 5)
 
     own_tile = lax.div(7 * k, 4)
-    wide_stream[:, pl.ds(0, D)] = stream
     wide_stream[:, pl.ds(D, 512)] = jnp.zeros((8, 512), F32)
     own_stream = wide_stream[:, pl.ds(pl.multiple_of(own_tile * 128, 128), 512)]
     own_stream = pltpu.roll(own_stream, lax.rem(512 - (OUT_COLS * k - 128 * own_tile), 512), 1)[:, :256]
@@ -371,6 +392,7 @@
             pltpu.SemaphoreType.DMA((HERE, CHUNKS)),
             pltpu.SemaphoreType.DMA((7,)),
             pltpu.SemaphoreType.DMA((7,)),
+            pltpu.SemaphoreType.DMA((2,)),
         ],
         compiler_params=pltpu.CompilerParams(
             collective_id=0, has_side_effects=True, vmem_limit_bytes=60 * 1024 * 1024

time: 49.5 us -> 49.1 us (level)
  no operation moved by 1% of the time
where the time goes in v7:
time: 49.1 us; the launch traced here: 48.9 us
  Pallas kernels  47.7 us (97%)
  local copies, waits for them, and re-layouts  1.26 us (3%)
    pallas_call x1, Pallas kernels, body(): pl.pallas_call(kernel, out_shape=jax.ShapeDtypeStruct((HERE, OUT_COLS), F...  47.7 us
    unnamed x1, local copies, waits for them, and re-layouts  1.26 us

profile of v7, /device:TPU:1, one launch (start us, length us, event | category | flops | bytes accessed | tf_op | source)
XLA Modules:
  0.0 48.9 jit_solution(17526785388414260847)
XLA Ops:
  0.0 47.7 %shard_map.109 = f32[2,224]{1,0:T(2,128)} custom-call(bf16[2,576,128]{2,1,0:T(8,128)(2,1)} %bitcast.7, bf16[2,576,5120]{2,1,0:T(8,128)(2,1)} %bitcast.4, bf16[2,576]{1,0:T(2,128)(2,1)} %new_hbm.1, s32[2]{0:T(128)} %lengths_ref.1, bf16[4,512,128]{2,1,0:T(8,128)(2,1)} %uv_hbm.1, bf16[512,7168]{1,0:T(8,128)(2,1)} %wo_hbm.1, bf16[2,7168]{1,0:T(2,128)(2,1)} %hid_hbm.1, ...), custom_call_target="tpu_custom_call" | custom-call | tf_op jit(solution)/shard_map/pallas_call | solution.py:357
  47.7 1.3 %copy.13 = f32[2,224]{1,0:T(2,128)} copy(f32[2,224]{1,0:T(2,128)} %shard_map.109) | data formatting | bytes 3584

commit v8 on v7

--- a/solution.py
+++ b/solution.py
@@ -272,7 +272,7 @@
     for copy in weights[2:4]:
         copy.wait()
     squares = jnp.zeros((8, 128), F32)
-    gate_proj = up_proj = jnp.zeros((8, LOCAL_FF), F32)
+    gate_proj = up_proj = jnp.zeros((LOCAL_FF, 8), F32)
     for g in range(2):
         low = 7 * g
         owner = jnp.logical_and(reducer, jnp.logical_and(own_chip >= low, own_chip < low + 7))
@@ -293,11 +293,11 @@
         stream = jnp.concatenate(tiles, axis=1)
         wide_stream[:, cols] = stream
         scaled = (stream * gain[cols].astype(F32).reshape(1, 3584)).astype(BF16)
-        gate_proj = gate_proj + dot(scaled, wg[:, cols], ((1,), (1,)))
-        up_proj = up_proj + dot(scaled, wu[:, cols], ((1,), (1,)))
+        gate_proj = gate_proj + dot(wg[:, cols], scaled, ((1,), (1,)))
+        up_proj = up_proj + dot(wu[:, cols], scaled, ((1,), (1,)))
     rstd = lax.rsqrt(jnp.sum(squares, axis=1, keepdims=True) * (1.0 / D) + 1e-06)
-    gate_proj = gate_proj * rstd
-    hidden = (gate_proj / (1.0 + jnp.exp(-gate_proj)) * (up_proj * rstd)).astype(BF16)
+    gate_proj, up_proj = gate_proj.T * rstd, up_proj.T * rstd
+    hidden = (gate_proj / (1.0 + jnp.exp(-gate_proj)) * up_proj).astype(BF16)
     weights[4].wait()
     own_half, in_half = lax.div(k, 16), lax.rem(k, 16)
     for own, first in enumerate((16 - 16 * own_half, 16 * own_half)):

time: 49.1 us -> 49.2 us (level)
  no operation moved by 1% of the time
where the time goes in v8:
time: 49.2 us; the launch traced here: 49.1 us
  Pallas kernels  47.8 us (97%)
  local copies, waits for them, and re-layouts  1.26 us (3%)
    pallas_call x1, Pallas kernels, body(): pl.pallas_call(kernel, out_shape=jax.ShapeDtypeStruct((HERE, OUT_COLS), F...  47.8 us
    unnamed x1, local copies, waits for them, and re-layouts  1.26 us

profile of v8, /device:TPU:1, one launch (start us, length us, event | category | flops | bytes accessed | tf_op | source)
XLA Modules:
  0.0 49.1 jit_solution(15482100862132647598)
XLA Ops:
  0.0 47.8 %shard_map.109 = f32[2,224]{1,0:T(2,128)} custom-call(bf16[2,576,128]{2,1,0:T(8,128)(2,1)} %bitcast.7, bf16[2,576,5120]{2,1,0:T(8,128)(2,1)} %bitcast.4, bf16[2,576]{1,0:T(2,128)(2,1)} %new_hbm.1, s32[2]{0:T(128)} %lengths_ref.1, bf16[4,512,128]{2,1,0:T(8,128)(2,1)} %uv_hbm.1, bf16[512,7168]{1,0:T(8,128)(2,1)} %wo_hbm.1, bf16[2,7168]{1,0:T(2,128)(2,1)} %hid_hbm.1, ...), custom_call_target="tpu_custom_call" | custom-call | tf_op jit(solution)/shard_map/pallas_call | solution.py:357
  47.8 1.3 %copy.13 = f32[2,224]{1,0:T(2,128)} copy(f32[2,224]{1,0:T(2,128)} %shard_map.109) | data formatting | bytes 3584
